TPU v7x, 256 devices: a whole 4x4x8 slice. The times are simulated.
256 devices in a mesh: expert: 2 (over core), grp: 4 (over y), blk: 8 (over z_hi, x), head: 4 (over z_lo).
Axes of the slice: x: 4, y: 4, z: 8 (z_hi: 2, z_lo: 4; z = z_hi * 4 + z_lo), core: 2. Of those that a mesh axis runs over, the one named last changes fastest.
Arguments:
- queries: bfloat16 [2, 20480, 4096], P('expert', ('grp', 'blk', 'head')), parts along dimension 1, may hold values from -64 to 64
- keys: bfloat16 [2, 20480, 4096], P('expert', ('grp', 'blk', 'head')), parts along dimension 1, may hold values from -10 to 10
- values: bfloat16 [2, 20480, 4096], P('expert', ('grp', 'blk', 'head')), parts along dimension 1, may hold values from -6 to 6
- readout: bfloat16 [2, 4096, 64], P('expert'), may hold values from -0.375 to 0.375
- latents: float32 [128, 5120, 64], P('grp', ('blk', 'head')), parts along dimension 0, may hold values from -6 to 6
- valid: int32 [128], P('grp'), parts along dimension 0, may hold values from 2560 to 5120, as said below
- assignment: int32 [8], P('grp'), parts along dimension 0, may hold values from 0 to 31, as said below
- steps: int32 [8], P('grp'), parts along dimension 0, may hold values from 9 to 39, as said below
Outputs:
- attended: bfloat16 [2, 20480, 4096], P('expert', ('grp', 'blk', 'head')), parts along dimension 1
- next_latents: float32 [2, 20480, 64], P('expert', ('grp', 'blk', 'head')), parts along dimension 1
There are 4 independent parts, one for each index of `grp`. A program takes and returns all parts, laid end to end along the dimension named above; an argument that names none is the same for every part. Nothing has to cross between parts.
Inputs may be any that keep to these rules, and one draw needn't show every extreme that they name: At least one queued clip has all 5120 tokens valid. `assignment`: two different clips, one of them the last queued clip 32 - 1; entry 0 goes to the high-noise expert, entry 1 to the low-noise one. `steps`: entry 0 is the last step before the switch to the low-noise expert; entry 1 is the sampler's last step, 39.
All inputs are finite; a program needn't handle non-finite values.
Results may differ from a plain program's by a relative error of at most 0.0065.
Values may be sent and summed in bfloat16 or wider, within the bound.
A program may use at most 256 MiB of HBM per device.

v0:
```python
import jax
import jax.numpy as jnp
from jax import lax
from jax.sharding import PartitionSpec as P

HD = 128
STEPS = 40


flow_shift = 5.0
masked_score = -1e30


def from_behind(block, axis, distance):
    devices = range(lax.axis_size(axis))
    route = [((i - distance) % len(devices), i) for i in devices]
    return lax.ppermute(block, axis, route)


def from_partner(block, axis, bit):
    count = lax.axis_size(axis)
    route = []
    for low in range(count):
        high = low | 1 << bit
        if high != low and high < count:
            route += [(low, high), (high, low)]
    return lax.ppermute(block, axis, route)


def noise_level(step_value):
    fraction = 1.0 - step_value.astype(jnp.float32) / STEPS
    return flow_shift * fraction / (1.0 + (flow_shift - 1.0) * fraction)


def fresh_state(row_count, head_count):
    return (
        jnp.full((head_count, row_count), masked_score, jnp.float32),
        jnp.zeros((head_count, row_count), jnp.float32),
        jnp.zeros((head_count, row_count, HD), jnp.float32),
    )


def absorb(running, query_rows, key_rows, value_rows, key_start, valid_count):
    running_max, row_total, weighted = running
    head_count = query_rows.shape[1] // HD
    query_split = query_rows.reshape(query_rows.shape[0], head_count, HD)
    key_split = key_rows.reshape(key_rows.shape[0], head_count, HD)
    value_split = value_rows.reshape(value_rows.shape[0], head_count, HD)
    scores = jnp.einsum(
        "qhd,khd->hqk", query_split, key_split, preferred_element_type=jnp.float32
    ) * HD ** (-0.5)
    positions = key_start + lax.iota(jnp.int32, key_rows.shape[0])
    usable = (positions < valid_count)[None, None, :]
    scores = jnp.where(usable, scores, masked_score)
    new_max = jnp.maximum(running_max, jnp.max(scores, axis=2))
    weights = jnp.where(usable, jnp.exp(scores - new_max[:, :, None]), 0.0)
    factor = jnp.exp(running_max - new_max)
    row_total = row_total * factor + jnp.sum(weights, axis=2)
    update = jnp.einsum(
        "hqk,khd->hqd",
        weights.astype(jnp.bfloat16),
        value_split,
        preferred_element_type=jnp.float32,
    )
    weighted = weighted * factor[:, :, None] + update
    return (new_max, row_total, weighted)


def finish(running, query_start, valid_count):
    running_max, row_total, weighted = running
    outputs = weighted / row_total[:, :, None]
    outputs = jnp.transpose(outputs, (1, 0, 2))
    positions = query_start + lax.iota(jnp.int32, outputs.shape[0])
    outputs = jnp.where((positions < valid_count)[:, None, None], outputs, 0.0)
    return outputs.astype(jnp.bfloat16).reshape(
        outputs.shape[0], outputs.shape[1] * outputs.shape[2]
    )


def local(queries, keys, values, readout, latents, valid, assignment, steps):
    section_index = lax.axis_index("expert")
    clip_index = assignment[section_index]
    valid_count = valid[clip_index]
    query_local = queries[0]
    key_local = keys[0]
    value_local = values[0]
    query_block, key_block, value_block = (
        lax.all_to_all(query_local, "head", split_axis=1, concat_axis=0, tiled=True),
        lax.all_to_all(key_local, "head", split_axis=1, concat_axis=0, tiled=True),
        lax.all_to_all(value_local, "head", split_axis=1, concat_axis=0, tiled=True),
    )
    row_count = query_block.shape[0]
    head_count = query_block.shape[1] // HD
    cycle_size = lax.axis_size("blk")
    cycle_index = lax.axis_index("blk")
    initial = fresh_state(row_count, head_count)

    def cycle_turn(turn_index, loop_state):
        running, key_now, value_now = loop_state
        source = (cycle_index - turn_index) % cycle_size
        running = absorb(running, query_block, key_now, value_now, source * row_count, valid_count)
        key_now, value_now = from_behind((key_now, value_now), "blk", 1)
        return (running, key_now, value_now)

    running, key_now, value_now = lax.fori_loop(
        0, cycle_size - 1, cycle_turn, (initial, key_block, value_block)
    )
    source = (cycle_index - (cycle_size - 1)) % cycle_size
    running = absorb(running, query_block, key_now, value_now, source * row_count, valid_count)
    attended_heads = finish(running, cycle_index * row_count, valid_count)
    merged = lax.all_to_all(attended_heads, "head", split_axis=0, concat_axis=1, tiled=True)
    velocity = jnp.dot(merged, readout[0], preferred_element_type=jnp.float32)
    latent = lax.dynamic_index_in_dim(latents, clip_index, 0, keepdims=False)
    step_value = steps[section_index]
    advanced = latent + (noise_level(step_value + 1) - noise_level(step_value)) * velocity
    handed = from_partner(advanced.astype(jnp.bfloat16), "expert", 0).astype(advanced.dtype)
    return (merged[None], handed[None])


def solution(mesh):
    placed = (
        P("expert", ("grp", "blk", "head"), None),
        P("expert", ("grp", "blk", "head"), None),
        P("expert", ("grp", "blk", "head"), None),
        P("expert", None, None),
        P("grp", ("blk", "head"), None),
        P("grp"),
        P("grp"),
        P("grp"),
    )
    return jax.shard_map(
        local,
        mesh=mesh,
        in_specs=placed,
        out_specs=(
            P("expert", ("grp", "blk", "head"), None),
            P("expert", ("grp", "blk", "head"), None),
        ),
        check_vma=False,
    )
```

profile of v0, /device:TPU:1, one launch (start us, length us, event | category | flops | bytes accessed | tf_op | source)
XLA Modules:
  0.0 978.7 jit_solution(8306934854861449826)
XLA Ops:
  16.5 26.2 %all-to-all-done.2 = bf16[160,4,1024]{2,0,1:T(8,128)(2,1)S(1)} async-done(((bf16[160,4,1024]{2,0,1:T(8,128)(2,1)}), bf16[160,4,1024]{2,0,1:T(8,128)(2,1)S(1)}, u32[]{:S(2)}, u32[]{:S(2)}) %all-to-all-start.2) | async-done | bytes 1310752 | tf_op jit(solution)/shard_map/all_to_all | solution.py:88
  53.2 23.8 %all-to-all-done = bf16[160,4,1024]{2,0,1:T(8,128)(2,1)S(1)} async-done(((bf16[160,4,1024]{2,0,1:T(8,128)(2,1)}), bf16[160,4,1024]{2,0,1:T(8,128)(2,1)S(1)}, u32[]{:S(2)}, u32[]{:S(2)}) %all-to-all-start) | async-done | bytes 1310752 | tf_op jit(solution)/shard_map/all_to_all | solution.py:89
  87.1 24.3 %all-to-all-done.1 = bf16[160,4,1024]{2,0,1:T(8,128)(2,1)S(1)} async-done(((bf16[160,4,1024]{2,0,1:T(8,128)(2,1)}), bf16[160,4,1024]{2,0,1:T(8,128)(2,1)S(1)}, u32[]{:S(2)}, u32[]{:S(2)}) %all-to-all-start.1) | async-done | bytes 1310752 | tf_op jit(solution)/shard_map/all_to_all | solution.py:90
  111.4 811.3 %while.24 = (s32[]{:T(128)}, f32[8,640]{1,0:T(8,128)S(1)}, f32[8,640]{1,0:T(8,128)S(1)}, f32[8,640,128]{2,1,0:T(8,128)}, bf16[640,1024]{1,0:T(8,128)(2,1)S(1)}, ...) while((s32[]{:T(128)}, f32[8,640]{1,0:T(8,128)S(1)}, ...), condition=%wide.region_3.4_spmd.clone, body=%wide.region_0.3_spmd.clone.sunk | while | flops 1722312960 | bytes 116984704 | solution.py:105
  136.2 50.7 %collective-permute-done = bf16[640,1024]{1,0:T(8,128)(2,1)S(1)} collective-permute-done((bf16[640,1024]{1,0:T(8,128)(2,1)}, bf16[640,1024]{1,0:T(8,128)(2,1)S(1)}, u32[]{:S(2)}, u32[]{:S(2)}) %collective-permute-start) | collective-permute-done | bytes 1310752 | tf_op jit(solution)/shard_map/while/body/eval_jaxpr/ppermute | solution.py:17
  186.9 45.5 %collective-permute-done.1 = bf16[640,1024]{1,0:T(8,128)(2,1)S(1)} collective-permute-done((bf16[640,1024]{1,0:T(8,128)(2,1)}, bf16[640,1024]{1,0:T(8,128)(2,1)S(1)}, u32[]{:S(2)}, u32[]{:S(2)}) %collective-permute-start.1) | collective-permute-done | bytes 1310752 | tf_op jit(solution)/shard_map/while/body/eval_jaxpr/ppermute | solution.py:17
  243.8 11.8 %fusion.68 = f32[8,640,128]{2,1,0:T(8,128)} fusion(f32[8,640,128]{2,1,0:T(8,128)} %get-tuple-element.370, f32[8,640,640]{1,2,0:T(8,128)} %copy-done.1, f32[8,640]{1,0:T(8,128)S(1)} %select_maximum_fusion.2, pred[640]{0:T(1024)(128)(4,1)S(1)} %add_compare_fusion.4, f32[8,640]{1,0:T(8,128)S(1)} %get-tuple-element.352, pred[]{:T(512)S(6)} %compare.5, ...), kind=kOutput, calls=%fused_computation.8.clone.1 | convolution fusion | flops 857210880 | bytes 19702400 | tf_op jit(solution)/shard_map/while/body/eval_jaxpr/hqk,khd->hqd/dot_general | solution.py:59
  255.5 65.7 %collective-permute-done = bf16[640,1024]{1,0:T(8,128)(2,1)S(1)} collective-permute-done((bf16[640,1024]{1,0:T(8,128)(2,1)}, bf16[640,1024]{1,0:T(8,128)(2,1)S(1)}, u32[]{:S(2)}, u32[]{:S(2)}) %collective-permute-start) | collective-permute-done | bytes 1310752 | tf_op jit(solution)/shard_map/while/body/eval_jaxpr/ppermute | solution.py:17
  321.2 28.6 %collective-permute-done.1 = bf16[640,1024]{1,0:T(8,128)(2,1)S(1)} collective-permute-done((bf16[640,1024]{1,0:T(8,128)(2,1)}, bf16[640,1024]{1,0:T(8,128)(2,1)S(1)}, u32[]{:S(2)}, u32[]{:S(2)}) %collective-permute-start.1) | collective-permute-done | bytes 1310752 | tf_op jit(solution)/shard_map/while/body/eval_jaxpr/ppermute | solution.py:17
  361.2 11.8 %fusion.68 = f32[8,640,128]{2,1,0:T(8,128)} fusion(f32[8,640,128]{2,1,0:T(8,128)} %get-tuple-element.370, f32[8,640,640]{1,2,0:T(8,128)} %copy-done.1, f32[8,640]{1,0:T(8,128)S(1)} %select_maximum_fusion.2, pred[640]{0:T(1024)(128)(4,1)S(1)} %add_compare_fusion.4, f32[8,640]{1,0:T(8,128)S(1)} %get-tuple-element.352, pred[]{:T(512)S(6)} %compare.5, ...), kind=kOutput, calls=%fused_computation.8.clone.1 | convolution fusion | flops 857210880 | bytes 19702400 | tf_op jit(solution)/shard_map/while/body/eval_jaxpr/hqk,khd->hqd/dot_general | solution.py:59
  373.0 62.9 %collective-permute-done = bf16[640,1024]{1,0:T(8,128)(2,1)S(1)} collective-permute-done((bf16[640,1024]{1,0:T(8,128)(2,1)}, bf16[640,1024]{1,0:T(8,128)(2,1)S(1)}, u32[]{:S(2)}, u32[]{:S(2)}) %collective-permute-start) | collective-permute-done | bytes 1310752 | tf_op jit(solution)/shard_map/while/body/eval_jaxpr/ppermute | solution.py:17
  435.9 28.6 %collective-permute-done.1 = bf16[640,1024]{1,0:T(8,128)(2,1)S(1)} collective-permute-done((bf16[640,1024]{1,0:T(8,128)(2,1)}, bf16[640,1024]{1,0:T(8,128)(2,1)S(1)}, u32[]{:S(2)}, u32[]{:S(2)}) %collective-permute-start.1) | collective-permute-done | bytes 1310752 | tf_op jit(solution)/shard_map/while/body/eval_jaxpr/ppermute | solution.py:17
  475.9 11.8 %fusion.68 = f32[8,640,128]{2,1,0:T(8,128)} fusion(f32[8,640,128]{2,1,0:T(8,128)} %get-tuple-element.370, f32[8,640,640]{1,2,0:T(8,128)} %copy-done.1, f32[8,640]{1,0:T(8,128)S(1)} %select_maximum_fusion.2, pred[640]{0:T(1024)(128)(4,1)S(1)} %add_compare_fusion.4, f32[8,640]{1,0:T(8,128)S(1)} %get-tuple-element.352, pred[]{:T(512)S(6)} %compare.5, ...), kind=kOutput, calls=%fused_computation.8.clone.1 | convolution fusion | flops 857210880 | bytes 19702400 | tf_op jit(solution)/shard_map/while/body/eval_jaxpr/hqk,khd->hqd/dot_general | solution.py:59
  487.7 63.1 %collective-permute-done = bf16[640,1024]{1,0:T(8,128)(2,1)S(1)} collective-permute-done((bf16[640,1024]{1,0:T(8,128)(2,1)}, bf16[640,1024]{1,0:T(8,128)(2,1)S(1)}, u32[]{:S(2)}, u32[]{:S(2)}) %collective-permute-start) | collective-permute-done | bytes 1310752 | tf_op jit(solution)/shard_map/while/body/eval_jaxpr/ppermute | solution.py:17
  550.8 28.6 %collective-permute-done.1 = bf16[640,1024]{1,0:T(8,128)(2,1)S(1)} collective-permute-done((bf16[640,1024]{1,0:T(8,128)(2,1)}, bf16[640,1024]{1,0:T(8,128)(2,1)S(1)}, u32[]{:S(2)}, u32[]{:S(2)}) %collective-permute-start.1) | collective-permute-done | bytes 1310752 | tf_op jit(solution)/shard_map/while/body/eval_jaxpr/ppermute | solution.py:17
  590.7 11.8 %fusion.68 = f32[8,640,128]{2,1,0:T(8,128)} fusion(f32[8,640,128]{2,1,0:T(8,128)} %get-tuple-element.370, f32[8,640,640]{1,2,0:T(8,128)} %copy-done.1, f32[8,640]{1,0:T(8,128)S(1)} %select_maximum_fusion.2, pred[640]{0:T(1024)(128)(4,1)S(1)} %add_compare_fusion.4, f32[8,640]{1,0:T(8,128)S(1)} %get-tuple-element.352, pred[]{:T(512)S(6)} %compare.5, ...), kind=kOutput, calls=%fused_computation.8.clone.1 | convolution fusion | flops 857210880 | bytes 19702400 | tf_op jit(solution)/shard_map/while/body/eval_jaxpr/hqk,khd->hqd/dot_general | solution.py:59
  602.5 62.9 %collective-permute-done = bf16[640,1024]{1,0:T(8,128)(2,1)S(1)} collective-permute-done((bf16[640,1024]{1,0:T(8,128)(2,1)}, bf16[640,1024]{1,0:T(8,128)(2,1)S(1)}, u32[]{:S(2)}, u32[]{:S(2)}) %collective-permute-start) | collective-permute-done | bytes 1310752 | tf_op jit(solution)/shard_map/while/body/eval_jaxpr/ppermute | solution.py:17
  665.4 28.6 %collective-permute-done.1 = bf16[640,1024]{1,0:T(8,128)(2,1)S(1)} collective-permute-done((bf16[640,1024]{1,0:T(8,128)(2,1)}, bf16[640,1024]{1,0:T(8,128)(2,1)S(1)}, u32[]{:S(2)}, u32[]{:S(2)}) %collective-permute-start.1) | collective-permute-done | bytes 1310752 | tf_op jit(solution)/shard_map/while/body/eval_jaxpr/ppermute | solution.py:17
  705.4 11.8 %fusion.68 = f32[8,640,128]{2,1,0:T(8,128)} fusion(f32[8,640,128]{2,1,0:T(8,128)} %get-tuple-element.370, f32[8,640,640]{1,2,0:T(8,128)} %copy-done.1, f32[8,640]{1,0:T(8,128)S(1)} %select_maximum_fusion.2, pred[640]{0:T(1024)(128)(4,1)S(1)} %add_compare_fusion.4, f32[8,640]{1,0:T(8,128)S(1)} %get-tuple-element.352, pred[]{:T(512)S(6)} %compare.5, ...), kind=kOutput, calls=%fused_computation.8.clone.1 | convolution fusion | flops 857210880 | bytes 19702400 | tf_op jit(solution)/shard_map/while/body/eval_jaxpr/hqk,khd->hqd/dot_general | solution.py:59
  717.2 63.1 %collective-permute-done = bf16[640,1024]{1,0:T(8,128)(2,1)S(1)} collective-permute-done((bf16[640,1024]{1,0:T(8,128)(2,1)}, bf16[640,1024]{1,0:T(8,128)(2,1)S(1)}, u32[]{:S(2)}, u32[]{:S(2)}) %collective-permute-start) | collective-permute-done | bytes 1310752 | tf_op jit(solution)/shard_map/while/body/eval_jaxpr/ppermute | solution.py:17
  780.3 28.6 %collective-permute-done.1 = bf16[640,1024]{1,0:T(8,128)(2,1)S(1)} collective-permute-done((bf16[640,1024]{1,0:T(8,128)(2,1)}, bf16[640,1024]{1,0:T(8,128)(2,1)S(1)}, u32[]{:S(2)}, u32[]{:S(2)}) %collective-permute-start.1) | collective-permute-done | bytes 1310752 | tf_op jit(solution)/shard_map/while/body/eval_jaxpr/ppermute | solution.py:17
  832.0 62.5 %collective-permute-done = bf16[640,1024]{1,0:T(8,128)(2,1)S(1)} collective-permute-done((bf16[640,1024]{1,0:T(8,128)(2,1)}, bf16[640,1024]{1,0:T(8,128)(2,1)S(1)}, u32[]{:S(2)}, u32[]{:S(2)}) %collective-permute-start) | collective-permute-done | bytes 1310752 | tf_op jit(solution)/shard_map/while/body/eval_jaxpr/ppermute | solution.py:17
  894.5 28.1 %collective-permute-done.1 = bf16[640,1024]{1,0:T(8,128)(2,1)S(1)} collective-permute-done((bf16[640,1024]{1,0:T(8,128)(2,1)}, bf16[640,1024]{1,0:T(8,128)(2,1)S(1)}, u32[]{:S(2)}, u32[]{:S(2)}) %collective-permute-start.1) | collective-permute-done | bytes 1310752 | tf_op jit(solution)/shard_map/while/body/eval_jaxpr/ppermute | solution.py:17
  943.4 28.9 %all-to-all-done.3 = bf16[4,160,1024]{2,1,0:T(8,128)(2,1)S(1)} async-done(((bf16[4,160,1024]{2,1,0:T(8,128)(2,1)}), bf16[4,160,1024]{2,1,0:T(8,128)(2,1)S(1)}, u32[]{:S(2)}, u32[]{:S(2)}) %all-to-all-start.3) | async-done | bytes 1310752 | tf_op jit(solution)/shard_map/all_to_all | solution.py:111
  (130 shorter events, 164.8 us)
Async XLA Ops:
  0.6 971.8 %copy-start = (bf16[1,4096,64]{1,2,0:T(8,128)(2,1)S(1)}, bf16[1,4096,64]{1,2,0:T(8,128)(2,1)}, u32[]{:S(2)}) copy-start(bf16[1,4096,64]{1,2,0:T(8,128)(2,1)} %param.13) | copy-start | bytes 1572868
  5.4 37.3 %all-to-all-start.2 = ((bf16[160,4,1024]{2,0,1:T(8,128)(2,1)}), bf16[160,4,1024]{2,0,1:T(8,128)(2,1)S(1)}, u32[]{:S(2)}, u32[]{:S(2)}) async-start(bf16[160,4,1024]{2,0,1:T(8,128)(2,1)} %copy.38), calls=%async_computation.2 | async-start | bytes 2621440 | tf_op jit(solution)/shard_map/all_to_all | solution.py:88
  42.7 34.3 %copy-start.2 = (bf16[160,4,1024]{2,0,1:T(8,128)(2,1)}, bf16[160,4,1024]{2,0,1:T(8,128)(2,1)S(1)}, u32[]{:S(2)}) copy-start(bf16[160,4,1024]{2,0,1:T(8,128)(2,1)S(1)} %all-to-all-done.2) | copy-start | bytes 3932164
  42.7 34.3 %all-to-all-start = ((bf16[160,4,1024]{2,0,1:T(8,128)(2,1)}), bf16[160,4,1024]{2,0,1:T(8,128)(2,1)S(1)}, u32[]{:S(2)}, u32[]{:S(2)}) async-start(bf16[160,4,1024]{2,0,1:T(8,128)(2,1)} %copy.36), calls=%async_computation | async-start | bytes 2621440 | tf_op jit(solution)/shard_map/all_to_all | solution.py:89
  50.4 30.5 %copy-start.3 = (s32[2]{0:T(128)S(1)}, s32[2]{0:T(128)}, u32[]{:S(2)}) copy-start(s32[2]{0:T(128)} %param.16) | copy-start | bytes 28
  50.4 32.8 %copy-start.4 = (s32[32]{0:T(128)S(1)}, s32[32]{0:T(128)}, u32[]{:S(2)}) copy-start(s32[32]{0:T(128)} %param.15) | copy-start | bytes 388
  77.0 34.3 %all-to-all-start.1 = ((bf16[160,4,1024]{2,0,1:T(8,128)(2,1)}), bf16[160,4,1024]{2,0,1:T(8,128)(2,1)S(1)}, u32[]{:S(2)}, u32[]{:S(2)}) async-start(bf16[160,4,1024]{2,0,1:T(8,128)(2,1)} %copy.37), calls=%async_computation.1 | async-start | bytes 2621440 | tf_op jit(solution)/shard_map/all_to_all | solution.py:90
  112.4 74.4 %collective-permute-start = (bf16[640,1024]{1,0:T(8,128)(2,1)}, bf16[640,1024]{1,0:T(8,128)(2,1)S(1)}, u32[]{:S(2)}, u32[]{:S(2)}) collective-permute-start(bf16[640,1024]{1,0:T(8,128)(2,1)} %copy.101), channel_id=1, source_target_pairs={{28,0},{0,4},{4,8},{8,12},{12,16},{16,20},{20,24},{24,28},{29,1},{... | collective-permute-start | bytes 3932168 | tf_op jit(solution)/shard_map/while/body/eval_jaxpr/ppermute | solution.py:17
  114.7 117.7 %collective-permute-start.1 = (bf16[640,1024]{1,0:T(8,128)(2,1)}, bf16[640,1024]{1,0:T(8,128)(2,1)S(1)}, u32[]{:S(2)}, u32[]{:S(2)}) collective-permute-start(bf16[640,1024]{1,0:T(8,128)(2,1)} %copy.102), channel_id=1, source_target_pairs={{28,0},{0,4},{4,8},{8,12},{12,16},{16,20},{20,24},{24,28},{29,1},{... | collective-permute-start | bytes 3932168 | tf_op jit(solution)/shard_map/while/body/eval_jaxpr/ppermute | solution.py:17
  233.5 87.8 %collective-permute-start = (bf16[640,1024]{1,0:T(8,128)(2,1)}, bf16[640,1024]{1,0:T(8,128)(2,1)S(1)}, u32[]{:S(2)}, u32[]{:S(2)}) collective-permute-start(bf16[640,1024]{1,0:T(8,128)(2,1)} %copy.101), channel_id=1, source_target_pairs={{28,0},{0,4},{4,8},{8,12},{12,16},{16,20},{20,24},{24,28},{29,1},{... | collective-permute-start | bytes 3932168 | tf_op jit(solution)/shard_map/while/body/eval_jaxpr/ppermute | solution.py:17
  234.5 115.3 %collective-permute-start.1 = (bf16[640,1024]{1,0:T(8,128)(2,1)}, bf16[640,1024]{1,0:T(8,128)(2,1)S(1)}, u32[]{:S(2)}, u32[]{:S(2)}) collective-permute-start(bf16[640,1024]{1,0:T(8,128)(2,1)} %copy.102), channel_id=1, source_target_pairs={{28,0},{0,4},{4,8},{8,12},{12,16},{16,20},{20,24},{24,28},{29,1},{... | collective-permute-start | bytes 3932168 | tf_op jit(solution)/shard_map/while/body/eval_jaxpr/ppermute | solution.py:17
  350.9 85.0 %collective-permute-start = (bf16[640,1024]{1,0:T(8,128)(2,1)}, bf16[640,1024]{1,0:T(8,128)(2,1)S(1)}, u32[]{:S(2)}, u32[]{:S(2)}) collective-permute-start(bf16[640,1024]{1,0:T(8,128)(2,1)} %copy.101), channel_id=1, source_target_pairs={{28,0},{0,4},{4,8},{8,12},{12,16},{16,20},{20,24},{24,28},{29,1},{... | collective-permute-start | bytes 3932168 | tf_op jit(solution)/shard_map/while/body/eval_jaxpr/ppermute | solution.py:17
  351.9 112.5 %collective-permute-start.1 = (bf16[640,1024]{1,0:T(8,128)(2,1)}, bf16[640,1024]{1,0:T(8,128)(2,1)S(1)}, u32[]{:S(2)}, u32[]{:S(2)}) collective-permute-start(bf16[640,1024]{1,0:T(8,128)(2,1)} %copy.102), channel_id=1, source_target_pairs={{28,0},{0,4},{4,8},{8,12},{12,16},{16,20},{20,24},{24,28},{29,1},{... | collective-permute-start | bytes 3932168 | tf_op jit(solution)/shard_map/while/body/eval_jaxpr/ppermute | solution.py:17
  465.6 85.2 %collective-permute-start = (bf16[640,1024]{1,0:T(8,128)(2,1)}, bf16[640,1024]{1,0:T(8,128)(2,1)S(1)}, u32[]{:S(2)}, u32[]{:S(2)}) collective-permute-start(bf16[640,1024]{1,0:T(8,128)(2,1)} %copy.101), channel_id=1, source_target_pairs={{28,0},{0,4},{4,8},{8,12},{12,16},{16,20},{20,24},{24,28},{29,1},{... | collective-permute-start | bytes 3932168 | tf_op jit(solution)/shard_map/while/body/eval_jaxpr/ppermute | solution.py:17
  466.6 112.7 %collective-permute-start.1 = (bf16[640,1024]{1,0:T(8,128)(2,1)}, bf16[640,1024]{1,0:T(8,128)(2,1)S(1)}, u32[]{:S(2)}, u32[]{:S(2)}) collective-permute-start(bf16[640,1024]{1,0:T(8,128)(2,1)} %copy.102), channel_id=1, source_target_pairs={{28,0},{0,4},{4,8},{8,12},{12,16},{16,20},{20,24},{24,28},{29,1},{... | collective-permute-start | bytes 3932168 | tf_op jit(solution)/shard_map/while/body/eval_jaxpr/ppermute | solution.py:17
  580.4 85.0 %collective-permute-start = (bf16[640,1024]{1,0:T(8,128)(2,1)}, bf16[640,1024]{1,0:T(8,128)(2,1)S(1)}, u32[]{:S(2)}, u32[]{:S(2)}) collective-permute-start(bf16[640,1024]{1,0:T(8,128)(2,1)} %copy.101), channel_id=1, source_target_pairs={{28,0},{0,4},{4,8},{8,12},{12,16},{16,20},{20,24},{24,28},{29,1},{... | collective-permute-start | bytes 3932168 | tf_op jit(solution)/shard_map/while/body/eval_jaxpr/ppermute | solution.py:17
  581.5 112.5 %collective-permute-start.1 = (bf16[640,1024]{1,0:T(8,128)(2,1)}, bf16[640,1024]{1,0:T(8,128)(2,1)S(1)}, u32[]{:S(2)}, u32[]{:S(2)}) collective-permute-start(bf16[640,1024]{1,0:T(8,128)(2,1)} %copy.102), channel_id=1, source_target_pairs={{28,0},{0,4},{4,8},{8,12},{12,16},{16,20},{20,24},{24,28},{29,1},{... | collective-permute-start | bytes 3932168 | tf_op jit(solution)/shard_map/while/body/eval_jaxpr/ppermute | solution.py:17
  695.1 85.2 %collective-permute-start = (bf16[640,1024]{1,0:T(8,128)(2,1)}, bf16[640,1024]{1,0:T(8,128)(2,1)S(1)}, u32[]{:S(2)}, u32[]{:S(2)}) collective-permute-start(bf16[640,1024]{1,0:T(8,128)(2,1)} %copy.101), channel_id=1, source_target_pairs={{28,0},{0,4},{4,8},{8,12},{12,16},{16,20},{20,24},{24,28},{29,1},{... | collective-permute-start | bytes 3932168 | tf_op jit(solution)/shard_map/while/body/eval_jaxpr/ppermute | solution.py:17
  696.1 112.7 %collective-permute-start.1 = (bf16[640,1024]{1,0:T(8,128)(2,1)}, bf16[640,1024]{1,0:T(8,128)(2,1)S(1)}, u32[]{:S(2)}, u32[]{:S(2)}) collective-permute-start(bf16[640,1024]{1,0:T(8,128)(2,1)} %copy.102), channel_id=1, source_target_pairs={{28,0},{0,4},{4,8},{8,12},{12,16},{16,20},{20,24},{24,28},{29,1},{... | collective-permute-start | bytes 3932168 | tf_op jit(solution)/shard_map/while/body/eval_jaxpr/ppermute | solution.py:17
  809.9 84.6 %collective-permute-start = (bf16[640,1024]{1,0:T(8,128)(2,1)}, bf16[640,1024]{1,0:T(8,128)(2,1)S(1)}, u32[]{:S(2)}, u32[]{:S(2)}) collective-permute-start(bf16[640,1024]{1,0:T(8,128)(2,1)} %copy.101), channel_id=1, source_target_pairs={{28,0},{0,4},{4,8},{8,12},{12,16},{16,20},{20,24},{24,28},{29,1},{... | collective-permute-start | bytes 3932168 | tf_op jit(solution)/shard_map/while/body/eval_jaxpr/ppermute | solution.py:17
  811.0 111.7 %collective-permute-start.1 = (bf16[640,1024]{1,0:T(8,128)(2,1)}, bf16[640,1024]{1,0:T(8,128)(2,1)S(1)}, u32[]{:S(2)}, u32[]{:S(2)}) collective-permute-start(bf16[640,1024]{1,0:T(8,128)(2,1)} %copy.102), channel_id=1, source_target_pairs={{28,0},{0,4},{4,8},{8,12},{12,16},{16,20},{20,24},{24,28},{29,1},{... | collective-permute-start | bytes 3932168 | tf_op jit(solution)/shard_map/while/body/eval_jaxpr/ppermute | solution.py:17
  936.4 5.0 copy-start.5
  937.8 34.5 %all-to-all-start.3 = ((bf16[4,160,1024]{2,1,0:T(8,128)(2,1)}), bf16[4,160,1024]{2,1,0:T(8,128)(2,1)S(1)}, u32[]{:S(2)}, u32[]{:S(2)}) async-start(bf16[4,160,1024]{2,1,0:T(8,128)(2,1)} %all_to_all.68), calls=%async_computation.3 | async-start | bytes 2621440 | tf_op jit(solution)/shard_map/all_to_all | solution.py:111
  973.9 4.2 collective-permute-start.2
  (8 other events, 36.6 us)
where the time goes:
time: 980 us; the launch traced here: 979 us
  waiting for transfers between devices  751 us (77%)
  matrix products  120 us (12%)
  local copies, waits for them, and re-layouts  48.3 us (5%)
  other arithmetic  34.5 us (4%)
  starting transfers between devices  21.1 us (2%)
    ppermute x14, waiting for transfers between devices, from_behind(): return lax.ppermute(block, axis, route)  647 us
    dot_general x8, matrix products, absorb(): jnp.einsum('hqk,khd->hqd', weights.astype(jnp.bfloat16), value_split, pre...  87.2 us
    dot_general x8, matrix products, absorb(): jnp.einsum('qhd,khd->hqk', query_split, key_split, preferred_element_type...  31.2 us
    reduce_sum x8, other arithmetic, absorb(): row_total = row_total * factor + jnp.sum(weights, axis=2)  29.1 us
    all_to_all x1, waiting for transfers between devices, local(): lax.all_to_all(attended_heads, 'head', split_axis=0, concat_axis=1, tiled...  28.9 us
    all_to_all x1, waiting for transfers between devices, local(): lax.all_to_all(query_local, 'head', split_axis=1, concat_axis=0, tiled=True)  26.2 us
    all_to_all x1, waiting for transfers between devices, local(): lax.all_to_all(value_local, 'head', split_axis=1, concat_axis=0, tiled=True)  24.3 us
    all_to_all x1, waiting for transfers between devices, local(): lax.all_to_all(key_local, 'head', split_axis=1, concat_axis=0, tiled=True)  23.8 us
  transfers between devices with their start and end apart: 19, of which 18 were waited for; matrix products, arithmetic and copies ran while one was open for 16% of the time, Pallas kernels for 0%

commit v1 on v0

v1 whole, which is shorter than its diff:
```python
import functools

import jax
import jax.numpy as jnp
import numpy as np
from jax import lax
from jax.experimental import pallas as pl
from jax.experimental.pallas import tpu as pltpu
from jax.sharding import PartitionSpec as P

MESH = pl.DeviceIdType.MESH
HD = 128
PC = 64
STEPS = 40
FLOW_SHIFT = 5.0
MASKED = -1e30
SCORE_SCALE = float(HD**-0.5 / np.log(2.0))

ROWS = 160
XS, ZS, ZLO = 4, 8, 4
DEVICES = XS * ZS
TOKENS = DEVICES * ROWS
PAIRS = DEVICES // 2
BLOCK = 2 * ROWS
KEY_CHUNK = 1280
CHUNKS = TOKENS // KEY_CHUNK


def offset_of(step, side):
    dx, turn = step % 4, step // 4
    near = 3 - turn - turn // 2 + 2 * (turn // 3)
    if side == 0:
        return dx, near
    return (4 - dx) % 4, 8 - near - 4 * (1 - (near + 3) // 4)


def kernel(
    valid_ref, assignment_ref, steps_ref, q_ref, k_ref, v_ref, readout_ref, latents_ref,
    attended_ref, next_ref,
    k_in, k_two, v_two, q_in, o_out, o_in, bias, score_a, score_b, map_in, latents_in, handed_out, handed_in,
    k_send, k_recv, v_send, v_recv, q_send, q_recv, o_send, o_recv, own_sem, out_sem, hand_sem,
):
    expert, blk, head = lax.axis_index("expert"), lax.axis_index("blk"), lax.axis_index("head")
    my_x, my_z = blk % XS, (blk // XS) * ZLO + head
    me = blk * ZLO + head

    def partner(step, side, sign):
        dx, dz = offset_of(step, side)
        x = (my_x + sign * dx + XS) % XS
        z = (my_z + sign * dz + ZS) % ZS
        other_blk, other_head = (z // ZLO) * XS + x, z % ZLO
        return {"blk": other_blk, "head": other_head}, other_blk * ZLO + other_head

    own_step = 8

    def columns(index):
        return pl.ds(pl.multiple_of(index * HD, HD), HD)

    def rows(start, count):
        return pl.ds(pl.multiple_of(start, 32), count)

    def slot(step, side):
        return rows(step * BLOCK + side * ROWS, ROWS)

    def each_partner(action):
        def one(step, carry):
            @pl.when(step != own_step)
            def _():
                action(step, 0)

            action(step, 1)
            return carry

        lax.fori_loop(0, PAIRS, one, 0)

    barrier = pltpu.get_barrier_semaphore()
    swap = {"expert": 1 - expert}

    def greet(step, side):
        device, _ = partner(step, side, -1)
        pl.semaphore_signal(barrier, inc=1, device_id=device, device_id_type=MESH)

    each_partner(greet)
    pl.semaphore_signal(barrier, inc=1, device_id=swap, device_id_type=MESH)
    pl.semaphore_wait(barrier, DEVICES)

    def send_k(step, side):
        device, index = partner(step, side, 1)
        pltpu.make_async_remote_copy(
            k_ref.at[0, :, columns(index)], k_in.at[rows(me * ROWS, ROWS)], k_send, k_recv,
            device_id=device, device_id_type=MESH,
        ).start()

    def send_v(step, side):
        device, index = partner(step, side, 1)
        pltpu.make_async_remote_copy(
            v_ref.at[0, :, columns(index)], v_two.at[rows(me * ROWS, ROWS), pl.ds(0, HD)], v_send, v_recv,
            device_id=device, device_id_type=MESH,
        ).start()

    def send_q(step, side):
        device, index = partner(step, side, 1)
        pltpu.make_async_remote_copy(
            q_ref.at[0, :, columns(index)], q_in.at[slot(step, side)], q_send, q_recv.at[step],
            device_id=device, device_id_type=MESH,
        ).start()

    each_partner(send_k)
    own_k = pltpu.make_async_copy(k_ref.at[0, :, columns(me)], k_in.at[rows(me * ROWS, ROWS)], own_sem.at[0])
    own_k.start()
    own_v = pltpu.make_async_copy(
        v_ref.at[0, :, columns(me)], v_two.at[rows(me * ROWS, ROWS), pl.ds(0, HD)], own_sem.at[1]
    )
    own_v.start()
    own_q = pltpu.make_async_copy(q_ref.at[0, :, columns(me)], q_in.at[slot(own_step, 0)], own_sem.at[2])
    own_q.start()
    each_partner(send_v)
    each_partner(send_q)

    map_copy = pltpu.make_async_copy(readout_ref.at[0], map_in, own_sem.at[3])
    map_copy.start()
    latents_copy = pltpu.make_async_copy(latents_ref, latents_in, own_sem.at[4])
    latents_copy.start()

    clip = assignment_ref[expert]
    count = valid_ref[clip]
    v_two[:, HD:] = jnp.ones((TOKENS, HD), jnp.bfloat16)
    position = lax.broadcasted_iota(jnp.int32, (8, TOKENS), 1)
    bias[...] = jnp.where(position < count, 0.0, MASKED)

    own_k.wait()
    pltpu.make_async_copy(k_in.at[pl.ds(0, TOKENS - ROWS)], k_in.at[pl.ds(0, TOKENS - ROWS)], k_recv).wait()
    turned = jnp.transpose(k_in[...])
    k_two[0:HD, :] = turned
    k_two[HD:, :] = turned

    def queries_of(step):
        @pl.when(step != own_step)
        def _():
            pltpu.make_async_copy(q_in.at[rows(0, BLOCK)], q_in.at[rows(0, BLOCK)], q_recv.at[step]).wait()

        @pl.when(step == own_step)
        def _():
            own_q.wait()
            pltpu.make_async_copy(q_in.at[rows(0, ROWS)], q_in.at[rows(0, ROWS)], q_recv.at[step]).wait()

        scaled = q_in[rows(step * BLOCK, BLOCK), :].astype(jnp.float32) * SCORE_SCALE
        high = scaled.astype(jnp.bfloat16)
        low = (scaled - high.astype(jnp.float32)).astype(jnp.bfloat16)
        return jnp.concatenate([high, low], axis=1)

    def score_chunk(query, chunk, score_ref, most):
        at = slice(chunk * KEY_CHUNK, (chunk + 1) * KEY_CHUNK)
        scores = jnp.dot(query, k_two[:, at], preferred_element_type=jnp.float32)
        if (chunk + 1) * KEY_CHUNK > TOKENS // 2:
            scores = scores + bias[0:1, at]
        score_ref[:, at] = scores
        for lane in range(0, KEY_CHUNK, HD):
            piece = scores[:, lane : lane + HD]
            most = piece if most is None else jnp.maximum(most, piece)
        return most

    def value_chunk(top, chunk, score_ref, total):
        at = slice(chunk * KEY_CHUNK, (chunk + 1) * KEY_CHUNK)
        weights = jnp.exp2(score_ref[:, at] - top).astype(jnp.bfloat16)
        update = jnp.dot(weights, v_two[at, :], preferred_element_type=jnp.float32)
        return update if total is None else total + update

    def finish(step, total):
        outputs = total[:, :HD] / total[:, HD:]
        for side in range(2):
            device, index = partner(step, side, -1)
            token = index * ROWS + lax.broadcasted_iota(jnp.int32, (ROWS, HD), 0)
            kept = jnp.where(token < count, outputs[side * ROWS : (side + 1) * ROWS], 0.0)
            o_out[slot(step, side), :] = kept.astype(jnp.bfloat16)

            def send(device=device, side=side):
                pltpu.make_async_remote_copy(
                    o_out.at[slot(step, side)], o_in.at[slot(step, side)], o_send, o_recv.at[step],
                    device_id=device, device_id_type=MESH,
                ).start()

            if side == 0:
                pl.when(step != own_step)(send)
            else:
                send()

    def scored(step, score_ref):
        query, most = queries_of(step), None
        for chunk in range(CHUNKS):
            most = score_chunk(query, chunk, score_ref, most)
        return jnp.max(most, axis=1, keepdims=True)

    def turn(step, top, now_ref, next_ref):
        query = queries_of(step + 1)
        most = total = None
        for chunk in range(CHUNKS):
            most = score_chunk(query, chunk, next_ref, most)
            total = value_chunk(top, chunk, now_ref, total)
        finish(step, total)
        return jnp.max(most, axis=1, keepdims=True)

    top = scored(0, score_a)
    own_v.wait()
    pltpu.make_async_copy(k_in.at[pl.ds(0, TOKENS - ROWS)], k_in.at[pl.ds(0, TOKENS - ROWS)], v_recv).wait()

    def two_turns(half, top):
        top = turn(2 * half, top, score_a, score_b)
        return turn(2 * half + 1, top, score_b, score_a)

    top = lax.fori_loop(0, PAIRS // 2 - 1, two_turns, top)
    top = turn(PAIRS - 2, top, score_a, score_b)
    total = None
    for chunk in range(CHUNKS):
        total = value_chunk(top, chunk, score_b, total)
    finish(PAIRS - 1, total)

    def collect(step, velocity):
        @pl.when(step != own_step)
        def _():
            pltpu.make_async_copy(o_in.at[rows(0, BLOCK)], o_in.at[rows(0, BLOCK)], o_recv.at[step]).wait()

        @pl.when(step == own_step)
        def _():
            pltpu.make_async_copy(o_in.at[rows(0, ROWS)], o_in.at[rows(0, ROWS)], o_recv.at[step]).wait()
            o_in[slot(own_step, 0), :] = o_out[slot(own_step, 0), :]

        for side in range(2):
            _, index = partner(step, side, 1)
            pltpu.make_async_copy(
                o_in.at[slot(step, side)], attended_ref.at[0, :, columns(index)], out_sem
            ).start()
            velocity = velocity + lax.dot_general(
                map_in[:, columns(index)], o_in[slot(step, side), :], (((1,), (1,)), ((), ())),
                preferred_element_type=jnp.float32,
            )
        return velocity

    map_copy.wait()
    velocity = lax.fori_loop(0, PAIRS, collect, jnp.zeros((PC, ROWS), jnp.float32))

    def noise_level(step_value):
        fraction = 1.0 - step_value.astype(jnp.float32) / STEPS
        return FLOW_SHIFT * fraction / (1.0 + (FLOW_SHIFT - 1.0) * fraction)

    at = jnp.full((PC, ROWS), steps_ref[expert], jnp.int32)
    latents_copy.wait()
    handed_out[...] = latents_in[clip] + (noise_level(at + 1) - noise_level(at)) * velocity
    hand = pltpu.make_async_remote_copy(
        handed_out, handed_in, hand_sem.at[0], hand_sem.at[1], device_id=swap, device_id_type=MESH
    )
    hand.start()

    def sent(sem):
        pltpu.make_async_copy(k_in.at[pl.ds(0, TOKENS - ROWS)], k_in.at[pl.ds(0, TOKENS - ROWS)], sem).wait()

    sent(k_send)
    sent(v_send)
    sent(q_send)
    sent(o_send)
    pltpu.make_async_copy(o_in, o_in, out_sem).wait()
    hand.wait()
    next_ref[0] = handed_in[...]


def local(queries, keys, values, readout, latents, valid, assignment, steps):
    anywhere = pl.BlockSpec(memory_space=pl.ANY)
    scalars = pl.BlockSpec(memory_space=pltpu.SMEM)
    inside = pl.BlockSpec(memory_space=pltpu.VMEM)
    bf16, f32 = jnp.bfloat16, jnp.float32
    dma = pltpu.SemaphoreType.DMA
    readout, latents = jnp.swapaxes(readout, 1, 2), jnp.swapaxes(latents, 1, 2)
    attended, advanced = pl.pallas_call(
        kernel,
        out_shape=(
            jax.ShapeDtypeStruct((1, ROWS, DEVICES * HD), bf16),
            jax.ShapeDtypeStruct((1, PC, ROWS), f32),
        ),
        in_specs=[scalars, scalars, scalars, anywhere, anywhere, anywhere, anywhere, anywhere],
        out_specs=(anywhere, inside),
        scratch_shapes=[
            pltpu.VMEM((TOKENS, HD), bf16),
            pltpu.VMEM((2 * HD, TOKENS), bf16),
            pltpu.VMEM((TOKENS, 2 * HD), bf16),
            pltpu.VMEM((TOKENS, HD), bf16),
            pltpu.VMEM((TOKENS, HD), bf16),
            pltpu.VMEM((TOKENS, HD), bf16),
            pltpu.VMEM((8, TOKENS), f32),
            pltpu.VMEM((BLOCK, TOKENS), f32),
            pltpu.VMEM((BLOCK, TOKENS), f32),
            pltpu.VMEM((PC, DEVICES * HD), bf16),
            pltpu.VMEM(latents.shape, f32),
            pltpu.VMEM((PC, ROWS), f32),
            pltpu.VMEM((PC, ROWS), f32),
            dma, dma, dma, dma, dma, dma((PAIRS,)), dma, dma((PAIRS,)), dma((5,)), dma, dma((2,)),
        ],
        compiler_params=pltpu.CompilerParams(
            collective_id=0, has_side_effects=True, vmem_limit_bytes=56 * 2**20
        ),
    )(valid, assignment, steps, queries, keys, values, readout, latents)
    return attended, jnp.swapaxes(advanced, 1, 2)


def solution(mesh):
    tokens = P("expert", ("grp", "blk", "head"), None)
    return jax.shard_map(
        local,
        mesh=mesh,
        in_specs=(
            tokens, tokens, tokens,
            P("expert", None, None),
            P("grp", ("blk", "head"), None),
            P("grp"), P("grp"), P("grp"),
        ),
        out_specs=(tokens, tokens),
        check_vma=False,
    )
```

time: 980 us -> 134 us (0.14)
  waiting for transfers between devices: 751 us -> 0 us
  Pallas kernels: 0 us -> 130 us
  matrix products: 120 us -> 0 us
  local copies, waits for them, and re-layouts: 48.3 us -> 3.16 us
  other arithmetic: 34.5 us -> 0 us
  starting transfers between devices: 21.1 us -> 0 us
    ppermute x15 -> x0, waiting for transfers between devices: 647 us -> none  [the longest x14 647 us: from_behind(): return lax.ppermute(block, axis, route)]
    pallas_call x0 -> x1, Pallas kernels: none -> 130 us  [local(): pl.pallas_call(kernel, out_shape=(jax.ShapeDtypeStruct((1, ROWS, DEVICES...]
    dot_general x17 -> x0, matrix products: 120 us -> none  [the longest x8 87.2 us: absorb(): jnp.einsum('hqk,khd->hqd', weights.astype(jnp.bfloat16), value_split, pre...]
    all_to_all x4 -> x0, waiting for transfers between devices: 103 us -> none  [the longest x1 28.9 us: local(): lax.all_to_all(attended_heads, 'head', split_axis=0, concat_axis=1, tiled...]
    reduce_sum x8 -> x0, other arithmetic: 29.1 us -> none  [absorb(): row_total = row_total * factor + jnp.sum(weights, axis=2)]
    while x35 -> x0, local copies, waits for them, and re-layouts: 22.2 us -> none
    all_to_all x9 -> x0, local copies, waits for them, and re-layouts: 18.9 us -> none  [the longest x2 6.95 us: local(): lax.all_to_all(value_local, 'head', split_axis=1, concat_axis=0, tiled=True)]
    all_to_all x4 -> x0, starting transfers between devices: 17.2 us -> none  [the longest x1 6.44 us: local(): lax.all_to_all(query_local, 'head', split_axis=1, concat_axis=0, tiled=True)]
  transfers between devices with their start and end apart: 19 -> 0, of which waited for: 18 -> 0; matrix products, arithmetic and copies ran while one was open for 16% -> 0% of each run, Pallas kernels for 0% -> 0%
where the time goes in v1:
time: 134 us
  Pallas kernels  130 us (97%)
  local copies, waits for them, and re-layouts  3.16 us (2%)
    pallas_call x1, Pallas kernels, local(): pl.pallas_call(kernel, out_shape=(jax.ShapeDtypeStruct((1, ROWS, DEVICES...  130 us
    unnamed x4, local copies, waits for them, and re-layouts  3.16 us

profile of v1, /device:TPU:1, one launch (start us, length us, event | category | flops | bytes accessed | tf_op | source)
XLA Modules:
  0.0 133.6 jit_solution(6134317792216019153)
XLA Ops:
  0.6 129.8 %shard_map.95 = (bf16[1,160,4096]{2,1,0:T(8,128)(2,1)}, f32[1,64,160]{2,1,0:T(8,128)}) custom-call(s32[32]{0:T(128)} %valid_ref.1, s32[2]{0:T(128)} %assignment_ref.1, s32[2]{0:T(128)} %steps_ref.1, bf16[1,160,4096]{2,1,0:T(8,128)(2,1)} %q_ref.1, bf16[1,160,4096]{2,1,0:T(8,128)(2,1)} %k_ref.1, bf16[1,160,4096]{2,1,0:T(8,128)(2,1)} %v_ref.1, ...), custom_call_target="tpu_custom_call" | custom-call | tf_op jit(solution)/shard_map/pallas_call | solution.py:273
  130.4 0.0 copy-start
  130.4 2.5 %copy.12 = bf16[1,160,4096]{2,1,0:T(8,128)(2,1)} copy(bf16[1,160,4096]{2,1,0:T(8,128)(2,1)} %get-tuple-element.8) | data formatting | bytes 2621440
  133.0 0.0 copy-done
  133.0 0.6 copy.13
Async XLA Ops:
  130.4 2.5 %copy-start = (f32[1,64,160]{2,1,0:T(8,128)S(1)}, f32[1,64,160]{2,1,0:T(8,128)}, u32[]{:S(2)}) copy-start(f32[1,64,160]{2,1,0:T(8,128)} %get-tuple-element.5) | copy-start | bytes 122884

commit v2 on v1

--- a/solution.py
+++ b/solution.py
@@ -36,9 +36,9 @@
 
 def kernel(
     valid_ref, assignment_ref, steps_ref, q_ref, k_ref, v_ref, readout_ref, latents_ref,
-    attended_ref, next_ref,
-    k_in, k_two, v_two, q_in, o_out, o_in, bias, score_a, score_b, map_in, latents_in, handed_out, handed_in,
-    k_send, k_recv, v_send, v_recv, q_send, q_recv, o_send, o_recv, own_sem, out_sem, hand_sem,
+    attended_ref, advanced_ref,
+    k_in, k_two, v_two, q_in, o_out, bias, score_a, score_b, map_in, latents_in,
+    k_send, k_recv, v_send, v_recv, q_send, q_recv, o_send, o_recv, own_sem, relay_sem,
 ):
     expert, blk, head = lax.axis_index("expert"), lax.axis_index("blk"), lax.axis_index("head")
     my_x, my_z = blk % XS, (blk // XS) * ZLO + head
@@ -73,16 +73,43 @@
 
         lax.fori_loop(0, PAIRS, one, 0)
 
+    def line_partners(action):
+        def along_z(turn, carry):
+            @pl.when(turn * 4 != own_step)
+            def _():
+                action(turn * 4, 0)
+
+            action(turn * 4, 1)
+            return carry
+
+        def along_x(dx, carry):
+            action(own_step + dx, 0)
+            return carry
+
+        lax.fori_loop(0, 4, along_z, 0)
+        lax.fori_loop(1, XS, along_x, 0)
+
+    def other_partners(action):
+        def one(at, carry):
+            step = (at // 3) * 4 + at % 3 + 1
+
+            @pl.when(at // 3 != own_step // 4)
+            def _():
+                action(step, 0)
+
+            action(step, 1)
+            return carry
+
+        lax.fori_loop(0, 12, one, 0)
+
     barrier = pltpu.get_barrier_semaphore()
-    swap = {"expert": 1 - expert}
 
     def greet(step, side):
         device, _ = partner(step, side, -1)
         pl.semaphore_signal(barrier, inc=1, device_id=device, device_id_type=MESH)
 
-    each_partner(greet)
-    pl.semaphore_signal(barrier, inc=1, device_id=swap, device_id_type=MESH)
-    pl.semaphore_wait(barrier, DEVICES)
+    line_partners(greet)
+    pl.semaphore_wait(barrier, XS + ZS - 2)
 
     def send_k(step, side):
         device, index = partner(step, side, 1)
@@ -105,7 +132,17 @@
             device_id=device, device_id_type=MESH,
         ).start()
 
-    each_partner(send_k)
+    line_partners(send_k)
+
+    def relay(dx, carry):
+        device, _ = partner(own_step + dx, 0, -1)
+        pl.semaphore_signal(relay_sem, inc=1, device_id=device, device_id_type=MESH)
+        return carry
+
+    lax.fori_loop(1, XS, relay, 0)
+    line_partners(send_v)
+    pl.semaphore_wait(relay_sem, XS - 1)
+    other_partners(send_k)
     own_k = pltpu.make_async_copy(k_ref.at[0, :, columns(me)], k_in.at[rows(me * ROWS, ROWS)], own_sem.at[0])
     own_k.start()
     own_v = pltpu.make_async_copy(
@@ -114,7 +151,7 @@
     own_v.start()
     own_q = pltpu.make_async_copy(q_ref.at[0, :, columns(me)], q_in.at[slot(own_step, 0)], own_sem.at[2])
     own_q.start()
-    each_partner(send_v)
+    other_partners(send_v)
     each_partner(send_q)
 
     map_copy = pltpu.make_async_copy(readout_ref.at[0], map_in, own_sem.at[3])
@@ -176,7 +213,7 @@
 
             def send(device=device, side=side):
                 pltpu.make_async_remote_copy(
-                    o_out.at[slot(step, side)], o_in.at[slot(step, side)], o_send, o_recv.at[step],
+                    o_out.at[slot(step, side)], attended_ref.at[0, :, columns(me)], o_send, o_recv.at[step],
                     device_id=device, device_id_type=MESH,
                 ).start()
 
@@ -218,20 +255,17 @@
     def collect(step, velocity):
         @pl.when(step != own_step)
         def _():
-            pltpu.make_async_copy(o_in.at[rows(0, BLOCK)], o_in.at[rows(0, BLOCK)], o_recv.at[step]).wait()
+            pltpu.make_async_copy(o_out.at[rows(0, BLOCK)], o_out.at[rows(0, BLOCK)], o_recv.at[step]).wait()
 
         @pl.when(step == own_step)
         def _():
-            pltpu.make_async_copy(o_in.at[rows(0, ROWS)], o_in.at[rows(0, ROWS)], o_recv.at[step]).wait()
-            o_in[slot(own_step, 0), :] = o_out[slot(own_step, 0), :]
+            pltpu.make_async_copy(o_out.at[rows(0, ROWS)], o_out.at[rows(0, ROWS)], o_recv.at[step]).wait()
+            attended_ref[0, :, columns(me)] = o_out[slot(own_step, 0), :]
 
         for side in range(2):
             _, index = partner(step, side, 1)
-            pltpu.make_async_copy(
-                o_in.at[slot(step, side)], attended_ref.at[0, :, columns(index)], out_sem
-            ).start()
             velocity = velocity + lax.dot_general(
-                map_in[:, columns(index)], o_in[slot(step, side), :], (((1,), (1,)), ((), ())),
+                map_in[:, columns(index)], attended_ref[0, :, columns(index)], (((1,), (1,)), ((), ())),
                 preferred_element_type=jnp.float32,
             )
         return velocity
@@ -245,11 +279,7 @@
 
     at = jnp.full((PC, ROWS), steps_ref[expert], jnp.int32)
     latents_copy.wait()
-    handed_out[...] = latents_in[clip] + (noise_level(at + 1) - noise_level(at)) * velocity
-    hand = pltpu.make_async_remote_copy(
-        handed_out, handed_in, hand_sem.at[0], hand_sem.at[1], device_id=swap, device_id_type=MESH
-    )
-    hand.start()
+    advanced_ref[0] = latents_in[clip] + (noise_level(at + 1) - noise_level(at)) * velocity
 
     def sent(sem):
         pltpu.make_async_copy(k_in.at[pl.ds(0, TOKENS - ROWS)], k_in.at[pl.ds(0, TOKENS - ROWS)], sem).wait()
@@ -258,9 +288,6 @@
     sent(v_send)
     sent(q_send)
     sent(o_send)
-    pltpu.make_async_copy(o_in, o_in, out_sem).wait()
-    hand.wait()
-    next_ref[0] = handed_in[...]
 
 
 def local(queries, keys, values, readout, latents, valid, assignment, steps):
@@ -273,16 +300,15 @@
     attended, advanced = pl.pallas_call(
         kernel,
         out_shape=(
-            jax.ShapeDtypeStruct((1, ROWS, DEVICES * HD), bf16),
-            jax.ShapeDtypeStruct((1, PC, ROWS), f32),
+            pltpu.VMEM((1, ROWS, DEVICES * HD), bf16),
+            pltpu.VMEM((1, PC, ROWS), f32),
         ),
         in_specs=[scalars, scalars, scalars, anywhere, anywhere, anywhere, anywhere, anywhere],
-        out_specs=(anywhere, inside),
+        out_specs=(inside, inside),
         scratch_shapes=[
             pltpu.VMEM((TOKENS, HD), bf16),
             pltpu.VMEM((2 * HD, TOKENS), bf16),
             pltpu.VMEM((TOKENS, 2 * HD), bf16),
-            pltpu.VMEM((TOKENS, HD), bf16),
             pltpu.VMEM((TOKENS, HD), bf16),
             pltpu.VMEM((TOKENS, HD), bf16),
             pltpu.VMEM((8, TOKENS), f32),
@@ -290,15 +316,15 @@
             pltpu.VMEM((BLOCK, TOKENS), f32),
             pltpu.VMEM((PC, DEVICES * HD), bf16),
             pltpu.VMEM(latents.shape, f32),
-            pltpu.VMEM((PC, ROWS), f32),
-            pltpu.VMEM((PC, ROWS), f32),
-            dma, dma, dma, dma, dma, dma((PAIRS,)), dma, dma((PAIRS,)), dma((5,)), dma, dma((2,)),
+            dma, dma, dma, dma, dma, dma((PAIRS,)), dma, dma((PAIRS,)), dma((5,)),
+            pltpu.SemaphoreType.REGULAR,
         ],
         compiler_params=pltpu.CompilerParams(
             collective_id=0, has_side_effects=True, vmem_limit_bytes=56 * 2**20
         ),
     )(valid, assignment, steps, queries, keys, values, readout, latents)
-    return attended, jnp.swapaxes(advanced, 1, 2)
+    handed = lax.ppermute(advanced, "expert", [(0, 1), (1, 0)])
+    return attended, jnp.swapaxes(handed, 1, 2)
 
 
 def solution(mesh):

time: 134 us -> 130 us (0.970)
  Pallas kernels: 130 us -> 126 us
  starting transfers between devices: 0 us -> 1.84 us
  local copies, waits for them, and re-layouts: 3.16 us -> 1.69 us
    pallas_call x1, Pallas kernels: 130 us -> 126 us  [local(): pl.pallas_call(kernel, out_shape=(pltpu.VMEM((1, ROWS, DEVICES * HD), bf1...]
    ppermute x0 -> x1, starting transfers between devices: none -> 1.84 us  [local(): handed = lax.ppermute(advanced, 'expert', [(0, 1), (1, 0)])]
    unnamed x4 -> x2, local copies, waits for them, and re-layouts: 3.16 us -> 1.69 us
  transfers between devices with their start and end apart: 0 -> 1, of which waited for: 0 -> 0; matrix products, arithmetic and copies ran while one was open for 0% -> 1% of each run, Pallas kernels for 0% -> 0%
where the time goes in v2:
time: 130 us
  Pallas kernels  126 us (97%)
  starting transfers between devices  1.84 us (1%)
  local copies, waits for them, and re-layouts  1.69 us (1%)
    pallas_call x1, Pallas kernels, local(): pl.pallas_call(kernel, out_shape=(pltpu.VMEM((1, ROWS, DEVICES * HD), bf1...  126 us
  transfers between devices with their start and end apart: 1, of which 0 were waited for; matrix products, arithmetic and copies ran while one was open for 1% of the time, Pallas kernels for 0%

profile of v2, /device:TPU:1, one launch (start us, length us, event | category | flops | bytes accessed | tf_op | source)
XLA Modules:
  0.0 129.7 jit_solution(14319536035420147167)
XLA Ops:
  0.6 125.6 %shard_map.95 = (bf16[1,160,4096]{2,1,0:T(8,128)(2,1)S(1)}, f32[1,64,160]{2,1,0:T(8,128)S(1)}) custom-call(s32[32]{0:T(128)} %valid_ref.1, s32[2]{0:T(128)} %assignment_ref.1, s32[2]{0:T(128)} %steps_ref.1, bf16[1,160,4096]{2,1,0:T(8,128)(2,1)} %q_ref.1, bf16[1,160,4096]{2,1,0:T(8,128)(2,1)} %k_ref.1, bf16[1,160,4096]{2,1,0:T(8,128)(2,1)} %v_ref.1, ...), custom_call_target="tpu_custom_call" | custom-call | tf_op jit(solution)/shard_map/pallas_call | solution.py:300
  126.2 1.8 %collective-permute-start = (f32[1,64,160]{2,1,0:T(8,128)S(1)}, f32[1,64,160]{2,1,0:T(8,128)S(1)}, u32[]{:S(2)}, u32[]{:S(2)}) collective-permute-start(f32[1,64,160]{2,1,0:T(8,128)S(1)} %get-tuple-element.5), channel_id=1, source_target_pairs={{0,128},{128,0},{1,129},{129,1},{2,130},{130,2},{3,131},{131,3},{4... | collective-permute-start | bytes 122888 | tf_op jit(solution)/shard_map/ppermute | solution.py:326
  128.0 1.1 copy.12
  129.1 0.0 collective-permute-done
  129.1 0.6 copy.13
Async XLA Ops:
  126.2 2.9 %collective-permute-start = (f32[1,64,160]{2,1,0:T(8,128)S(1)}, f32[1,64,160]{2,1,0:T(8,128)S(1)}, u32[]{:S(2)}, u32[]{:S(2)}) collective-permute-start(f32[1,64,160]{2,1,0:T(8,128)S(1)} %get-tuple-element.5), channel_id=1, source_target_pairs={{0,128},{128,0},{1,129},{129,1},{2,130},{130,2},{3,131},{131,3},{4... | collective-permute-start | bytes 122888 | tf_op jit(solution)/shard_map/ppermute | solution.py:326

commit v3 on v2

--- a/solution.py
+++ b/solution.py
@@ -28,7 +28,7 @@
 
 def offset_of(step, side):
     dx, turn = step % 4, step // 4
-    near = 3 - turn - turn // 2 + 2 * (turn // 3)
+    near = (turn + 1) % 4
     if side == 0:
         return dx, near
     return (4 - dx) % 4, 8 - near - 4 * (1 - (near + 3) // 4)
@@ -51,7 +51,7 @@
         other_blk, other_head = (z // ZLO) * XS + x, z % ZLO
         return {"blk": other_blk, "head": other_head}, other_blk * ZLO + other_head
 
-    own_step = 8
+    own_step = 12
 
     def columns(index):
         return pl.ds(pl.multiple_of(index * HD, HD), HD)

time: 130 us -> 128 us (0.985)
  Pallas kernels: 126 us -> 122 us
    pallas_call x1, Pallas kernels: 126 us -> 122 us  [local(): pl.pallas_call(kernel, out_shape=(pltpu.VMEM((1, ROWS, DEVICES * HD), bf1...]
where the time goes in v3:
time: 128 us; the launch traced here: 127 us
  Pallas kernels  122 us (95%)
  starting transfers between devices  3.12 us (2%)
  local copies, waits for them, and re-layouts  1.69 us (1%)
    pallas_call x1, Pallas kernels, local(): pl.pallas_call(kernel, out_shape=(pltpu.VMEM((1, ROWS, DEVICES * HD), bf1...  122 us
    ppermute x1, starting transfers between devices, local(): handed = lax.ppermute(advanced, 'expert', [(0, 1), (1, 0)])  3.12 us
  transfers between devices with their start and end apart: 1, of which 0 were waited for; matrix products, arithmetic and copies ran while one was open for 1% of the time, Pallas kernels for 0%

profile of v3, /device:TPU:1, one launch (start us, length us, event | category | flops | bytes accessed | tf_op | source)
XLA Modules:
  0.0 127.0 jit_solution(2146249743904272100)
XLA Ops:
  0.6 121.5 %shard_map.95 = (bf16[1,160,4096]{2,1,0:T(8,128)(2,1)S(1)}, f32[1,64,160]{2,1,0:T(8,128)S(1)}) custom-call(s32[32]{0:T(128)} %valid_ref.1, s32[2]{0:T(128)} %assignment_ref.1, s32[2]{0:T(128)} %steps_ref.1, bf16[1,160,4096]{2,1,0:T(8,128)(2,1)} %q_ref.1, bf16[1,160,4096]{2,1,0:T(8,128)(2,1)} %k_ref.1, bf16[1,160,4096]{2,1,0:T(8,128)(2,1)} %v_ref.1, ...), custom_call_target="tpu_custom_call" | custom-call | tf_op jit(solution)/shard_map/pallas_call | solution.py:300
  122.2 3.1 %collective-permute-start = (f32[1,64,160]{2,1,0:T(8,128)S(1)}, f32[1,64,160]{2,1,0:T(8,128)S(1)}, u32[]{:S(2)}, u32[]{:S(2)}) collective-permute-start(f32[1,64,160]{2,1,0:T(8,128)S(1)} %get-tuple-element.5), channel_id=1, source_target_pairs={{0,128},{128,0},{1,129},{129,1},{2,130},{130,2},{3,131},{131,3},{4... | collective-permute-start | bytes 122888 | tf_op jit(solution)/shard_map/ppermute | solution.py:326
  125.3 1.1 copy.12
  126.3 0.0 collective-permute-done
  126.3 0.6 copy.13
Async XLA Ops:
  122.2 4.2 %collective-permute-start = (f32[1,64,160]{2,1,0:T(8,128)S(1)}, f32[1,64,160]{2,1,0:T(8,128)S(1)}, u32[]{:S(2)}, u32[]{:S(2)}) collective-permute-start(f32[1,64,160]{2,1,0:T(8,128)S(1)} %get-tuple-element.5), channel_id=1, source_target_pairs={{0,128},{128,0},{1,129},{129,1},{2,130},{130,2},{3,131},{131,3},{4... | collective-permute-start | bytes 122888 | tf_op jit(solution)/shard_map/ppermute | solution.py:326
